TPU v7x, 32 devices: a whole 2x2x4 slice. The times are simulated.
32 devices in a mesh: group: 2 (over y), sub: 4 (over z), tile: 2 (over x), rep: 2 (over core).
Axes of the slice: x: 2, y: 2, z: 4, core: 2. Of those that a mesh axis runs over, the one named last changes fastest.
Arguments:
- right_side: bfloat16 [16, 1024, 512], P(('group', 'sub', 'tile'), None, 'rep'), parts along dimension 0, may hold values from -6 to 6
- interface_inverse: bfloat16 [16, 1024, 1024], P(('group', 'sub', 'tile')), parts along dimension 0, may hold values from -0.1875 to 0.1875
- coupling: float32 [16, 2, 128], P(('group', 'sub', 'tile')), parts along dimension 0, may hold values from 0.5 to 2
- trace_rows: int32 [16, 2, 128], P(('group', 'sub', 'tile')), parts along dimension 0, may hold values from 0 to 1023
- deflation_basis: bfloat16 [16, 1024, 128], P(('group', 'sub', 'tile')), parts along dimension 0, may hold values from -0.375 to 0.375
- deflation_counts: int32 [16], P(('group', 'sub', 'tile')), parts along dimension 0, may hold values from 32 to 128, as said below
- coarse_inverse: bfloat16 [8, 2, 128, 4, 256], P('group', 'tile', 'rep', 'sub'), parts along dimension 0, may hold values from -0.25 to 0.25
Outputs:
- corrected_field: bfloat16 [16, 1024, 512], P(('group', 'sub', 'tile'), None, 'rep'), parts along dimension 0
There are 2 independent parts, one for each index of `group`. A program takes and returns all parts, laid end to end along the dimension named above; each array names one. Nothing has to cross between parts.
Inputs may be any that keep to these rules, and one draw needn't show every extreme that they name: `deflation_counts`: some subdomain has exactly 128 live deflation vectors.
All inputs are finite; a program needn't handle non-finite values.
Results may differ from a plain program's by a relative error of at most 0.035.
Values may be sent and summed in bfloat16 or wider, within the bound.
A program may use at most 64 MiB of HBM per device.

v0:
```python
import jax
import jax.numpy as jnp
from jax import lax
from jax.sharding import PartitionSpec as P

ROUNDS = 2


def passed_along(shard, axis, by):
    peers = lax.axis_size(axis)
    pairs = [(i, i + by) for i in range(peers) if 0 <= i + by < peers]
    return lax.ppermute(shard, axis, pairs)


def add_columns(matrix, piece):
    return jnp.dot(matrix, piece, preferred_element_type=jnp.float32)


def local(
    right_side,
    interface_inverse,
    coupling,
    trace_rows,
    deflation_basis,
    deflation_counts,
    coarse_inverse,
):
    source = right_side[0].astype(jnp.float32)
    inverse = interface_inverse[0]
    iface_rows = inverse.shape[0]
    face_rows = coupling.shape[2]
    mode_cols = source.shape[1]
    slot_count = deflation_basis.shape[2]
    half_slots = coarse_inverse.shape[2]
    sub_count = lax.axis_size("sub")
    slot_ids = jnp.arange(slot_count, dtype=jnp.int32)
    masked_basis = jnp.where(
        slot_ids[None, :] < deflation_counts[0],
        deflation_basis[0],
        jnp.zeros((), deflation_basis.dtype),
    )
    coarse_block = coarse_inverse.reshape(sub_count * half_slots, coarse_inverse.shape[4])
    lower_gain = coupling[0, 0][:, None]
    upper_gain = coupling[0, 1][:, None]
    iterate = jnp.zeros((iface_rows, mode_cols), jnp.float32)
    for cycle_index in range(ROUNDS):
        lower_trace = iterate[trace_rows[0, 0]]
        upper_trace = iterate[trace_rows[0, 1]]
        from_lower = passed_along(upper_trace.astype(jnp.bfloat16), ("sub", "tile"), 1).astype(
            upper_trace.dtype
        )
        from_upper = passed_along(lower_trace.astype(jnp.bfloat16), ("sub", "tile"), -1).astype(
            lower_trace.dtype
        )
        lower_rows = source[:face_rows] + lower_gain * from_lower
        upper_rows = source[iface_rows - face_rows :] + upper_gain * from_upper
        boundary = jnp.concatenate(
            [lower_rows, source[face_rows : iface_rows - face_rows], upper_rows], axis=0
        ).astype(jnp.bfloat16)
        local_solve = jnp.dot(inverse, boundary, preferred_element_type=jnp.float32)
        defect = (local_solve - iterate).astype(jnp.bfloat16)
        projected = lax.dot_general(
            masked_basis, defect, (((0,), (0,)), ((), ())), preferred_element_type=jnp.float32
        ).astype(jnp.bfloat16)
        all_modes = lax.all_gather(projected, "rep", axis=1, tiled=True)
        partial_value = add_columns(
            coarse_block, lax.all_gather(all_modes, "tile", axis=0, tiled=True)
        )
        own_coarse = lax.psum_scatter(
            partial_value.astype(jnp.bfloat16), "sub", scatter_dimension=0, tiled=True
        )
        coarse_rows = lax.all_to_all(own_coarse, "rep", split_axis=1, concat_axis=0, tiled=True)
        iterate = local_solve + jnp.dot(
            masked_basis, coarse_rows, preferred_element_type=jnp.float32
        )
    return iterate.astype(jnp.bfloat16)[None]


def solution(mesh):
    placed = (
        P(("group", "sub", "tile"), None, "rep"),
        P(("group", "sub", "tile"), None, None),
        P(("group", "sub", "tile"), None, None),
        P(("group", "sub", "tile"), None, None),
        P(("group", "sub", "tile"), None, None),
        P(("group", "sub", "tile")),
        P("group", "tile", "rep", "sub", None),
    )
    return jax.shard_map(
        local,
        mesh=mesh,
        in_specs=placed,
        out_specs=P(("group", "sub", "tile"), None, "rep"),
        check_vma=False,
    )
```

profile of v0, /device:TPU:0, one launch (start us, length us, event | category | flops | bytes accessed | tf_op | source)
XLA Modules:
  0.0 124.2 jit_solution(14332137796741248323)
XLA Ops:
  8.3 4.8 %collective-permute-start = (bf16[128,256]{1,0:T(8,128)(2,1)S(1)}, bf16[128,256]{1,0:T(8,128)(2,1)S(1)}, u32[]{:S(2)}, u32[]{:S(2)}) collective-permute-start(bf16[128,256]{1,0:T(8,128)(2,1)S(1)} %gather_fusion), channel_id=1, source_target_pairs={{0,2},{2,4},{4,6},{6,8},{8,10},{10,12},{12,14},{1,3},{3,5},{5,7},{... | collective-permute-start | bytes 196616 | tf_op jit(solution)/shard_map/ppermute | solution.py:12
  14.0 1.3 %collective-permute-start.1 = (bf16[128,256]{1,0:T(8,128)(2,1)S(1)}, bf16[128,256]{1,0:T(8,128)(2,1)S(1)}, u32[]{:S(2)}, u32[]{:S(2)}) collective-permute-start(bf16[128,256]{1,0:T(8,128)(2,1)S(1)} %gather_fusion.1), channel_id=1, source_target_pairs={{2,0},{4,2},{6,4},{8,6},{10,8},{12,10},{14,12},{3,1},{5,3},{7,5},{... | collective-permute-start | bytes 196616 | tf_op jit(solution)/shard_map/ppermute | solution.py:12
  16.7 1.1 convert_element_type.57
  17.9 2.2 %collective-permute-done.1 = bf16[128,256]{1,0:T(8,128)(2,1)S(1)} collective-permute-done((bf16[128,256]{1,0:T(8,128)(2,1)S(1)}, bf16[128,256]{1,0:T(8,128)(2,1)S(1)}, u32[]{:S(2)}, u32[]{:S(2)}) %collective-permute-start.1) | collective-permute-done | bytes 65568 | tf_op jit(solution)/shard_map/ppermute | solution.py:12
  22.5 1.9 %all_gather.12 = bf16[128,512]{1,0:T(8,128)(2,1)S(1)} all-gather(bf16[128,256]{1,0:T(8,128)(2,1)S(1)} %convolution_convert_fusion.3), channel_id=1, replica_groups=mesh['group'=2,'sub'=4,'tile'=2,'rep'=2] {'rep'}, dimensions={1}, use_global_device_ids=true | all-gather | bytes 196608 | tf_op jit(solution)/shard_map/all_gather | solution.py:65
  24.4 6.9 %all_gather.13 = bf16[256,512]{1,0:T(8,128)(2,1)S(1)} all-gather(bf16[128,512]{1,0:T(8,128)(2,1)S(1)} %all_gather.12), channel_id=1, replica_groups=mesh['group'=2,'sub'=4,'tile'=2,'rep'=2] {'tile'}, dimensions={0}, use_global_device_ids=true | all-gather | bytes 393216 | tf_op jit(solution)/shard_map/all_gather | solution.py:67
  32.5 20.2 %reduce-scatter.7.cloned.1.call-done = bf16[64,512]{1,0:T(8,128)(2,1)} async-done(((bf16[256,512]{1,0:T(8,128)(2,1)}), bf16[64,512]{1,0:T(8,128)(2,1)}) %reduce-scatter.7.cloned.1.call-update) | async-done | bytes 65552
  53.7 3.8 %all_to_all.38 = bf16[64,2,256]{2,0,1:T(8,128)(2,1)S(1)} all-to-all(bf16[64,2,256]{2,0,1:T(8,128)(2,1)S(1)} %copy.35), channel_id=1, replica_groups=mesh['group'=2,'sub'=4,'tile'=2,'rep'=2] {'rep'}, dimensions={1} | all-to-all | bytes 131072 | tf_op jit(solution)/shard_map/all_to_all | solution.py:72
  57.5 1.6 %convolution_add_fusion.1 = f32[1024,256]{0,1:T(8,128)S(1)} fusion(f32[1024,256]{0,1:T(8,128)} %copy-done.1, bf16[128,256]{1,0:T(8,128)(2,1)S(1)} %bitcast.78, bf16[1,1024,128]{2,1,0:T(8,128)(2,1)S(1)} %copy-done.4, pred[128]{0:T(512)(128)(4,1)S(1)} %iota_compare_fusion), kind=kOutput, calls=%fused_computation.11 | convolution fusion | flops 67502080 | bytes 2424960 | tf_op jit(solution)/shard_map/dot_general | solution.py:73
  59.1 1.0 copy.37
  60.1 2.5 %gather_fusion.3 = bf16[128,256]{1,0:T(8,128)(2,1)} fusion(bf16[1024,256]{1,0:T(8,128)(2,1)} %copy.37, s32[1024]{0:T(1024)S(1)} %pad_clamp_fusion), kind=kCustom, calls=%fused_computation.3 | custom fusion | bytes 131584 | tf_op jit(solution)/shard_map/gather | solution.py:47
  62.6 2.5 %gather_fusion.2 = bf16[128,256]{1,0:T(8,128)(2,1)} fusion(bf16[1024,256]{1,0:T(8,128)(2,1)} %copy.37, s32[1024]{0:T(1024)S(1)} %pad_clamp_fusion.1), kind=kCustom, calls=%fused_computation.2 | custom fusion | bytes 131584 | tf_op jit(solution)/shard_map/gather | solution.py:48
  65.0 3.4 %collective-permute-start.2 = (bf16[128,256]{1,0:T(8,128)(2,1)}, bf16[128,256]{1,0:T(8,128)(2,1)S(1)}, u32[]{:S(2)}, u32[]{:S(2)}) collective-permute-start(bf16[128,256]{1,0:T(8,128)(2,1)} %gather_fusion.2), channel_id=1, source_target_pairs={{0,2},{2,4},{4,6},{6,8},{8,10},{10,12},{12,14},{1,3},{3,5},{5,7},{... | collective-permute-start | bytes 196616 | tf_op jit(solution)/shard_map/ppermute | solution.py:12
  68.5 1.3 %collective-permute-start.3 = (bf16[128,256]{1,0:T(8,128)(2,1)}, bf16[128,256]{1,0:T(8,128)(2,1)S(1)}, u32[]{:S(2)}, u32[]{:S(2)}) collective-permute-start(bf16[128,256]{1,0:T(8,128)(2,1)} %gather_fusion.3), channel_id=1, source_target_pairs={{2,0},{4,2},{6,4},{8,6},{10,8},{12,10},{14,12},{3,1},{5,3},{7,5},{... | collective-permute-start | bytes 196616 | tf_op jit(solution)/shard_map/ppermute | solution.py:12
  70.7 4.2 %collective-permute-done.3 = bf16[128,256]{1,0:T(8,128)(2,1)S(1)} collective-permute-done((bf16[128,256]{1,0:T(8,128)(2,1)}, bf16[128,256]{1,0:T(8,128)(2,1)S(1)}, u32[]{:S(2)}, u32[]{:S(2)}) %collective-permute-start.3) | collective-permute-done | bytes 65568 | tf_op jit(solution)/shard_map/ppermute | solution.py:12
  74.9 1.1 add_convert_fusion.1
  75.9 1.8 %fusion.7 = f32[1024,256]{0,1:T(8,128)S(1)} fusion(bf16[1,1024,1024]{2,1,0:T(8,128)(2,1)S(1)} %copy-done, bf16[768,256]{1,0:T(8,128)(2,1)} %copy-done.7, bf16[128,256]{1,0:T(8,128)(2,1)S(1)} %get-tuple-element.6, bf16[128,256]{1,0:T(8,128)(2,1)S(1)} %get-tuple-element.5), kind=kOutput, calls=%fused_computation.9 | convolution fusion | flops 538443776 | bytes 3670016 | tf_op jit(solution)/shard_map/dot_general | solution.py:60
  78.7 1.9 %all_gather.14 = bf16[128,512]{1,0:T(8,128)(2,1)S(1)} all-gather(bf16[128,256]{1,0:T(8,128)(2,1)S(1)} %convolution_convert_fusion.2), channel_id=1, replica_groups=mesh['group'=2,'sub'=4,'tile'=2,'rep'=2] {'rep'}, dimensions={1}, use_global_device_ids=true | all-gather | bytes 196608 | tf_op jit(solution)/shard_map/all_gather | solution.py:65
  80.6 6.4 %all_gather.15 = bf16[256,512]{1,0:T(8,128)(2,1)S(1)} all-gather(bf16[128,512]{1,0:T(8,128)(2,1)S(1)} %all_gather.14), channel_id=1, replica_groups=mesh['group'=2,'sub'=4,'tile'=2,'rep'=2] {'tile'}, dimensions={0}, use_global_device_ids=true | all-gather | bytes 393216 | tf_op jit(solution)/shard_map/all_gather | solution.py:67
  87.9 1.8 %copy.51 = bf16[256,512]{1,0:T(8,128)(2,1)} copy(bf16[256,512]{0,1:T(8,128)(2,1)} %fusion.13) | data formatting | bytes 524288
  89.7 18.1 %reduce-scatter.9.cloned.1.call-done = bf16[64,512]{1,0:T(8,128)(2,1)} async-done(((bf16[256,512]{1,0:T(8,128)(2,1)}), bf16[64,512]{1,0:T(8,128)(2,1)}) %reduce-scatter.9.cloned.1.call-update) | async-done | bytes 65552
  109.5 4.7 %all_to_all.39 = bf16[64,2,256]{2,0,1:T(8,128)(2,1)S(1)} all-to-all(bf16[64,2,256]{2,0,1:T(8,128)(2,1)} %copy.40), channel_id=1, replica_groups=mesh['group'=2,'sub'=4,'tile'=2,'rep'=2] {'rep'}, dimensions={1} | all-to-all | bytes 131072 | tf_op jit(solution)/shard_map/all_to_all | solution.py:72
  114.2 1.1 fusion.11
  115.3 2.0 %copy.42 = bf16[1,1024,256]{2,1,0:T(8,128)(2,1)} copy(bf16[1,1024,256]{1,2,0:T(8,128)(2,1)} %fusion.11) | data formatting | bytes 1048576 | tf_op jit(solution)/shard_map/broadcast_in_dim | solution.py:76
  (44 shorter events, 12.4 us)
Async XLA Ops:
  6.5 13.8 %copy-start = (bf16[1,1024,1024]{2,1,0:T(8,128)(2,1)S(1)}, bf16[1,1024,1024]{2,1,0:T(8,128)(2,1)}, u32[]{:S(2)}) copy-start(bf16[1,1024,1024]{2,1,0:T(8,128)(2,1)} %param.8) | copy-start | bytes 6291460
  6.5 46.1 %reduce-scatter.7.cloned.1.call-start = ((), (), s32[]{:S(2)}) async-start(), calls=%async_computation.4 | async-start | bytes 327680
  8.3 9.6 %collective-permute-start = (bf16[128,256]{1,0:T(8,128)(2,1)S(1)}, bf16[128,256]{1,0:T(8,128)(2,1)S(1)}, u32[]{:S(2)}, u32[]{:S(2)}) collective-permute-start(bf16[128,256]{1,0:T(8,128)(2,1)S(1)} %gather_fusion), channel_id=1, source_target_pairs={{0,2},{2,4},{4,6},{6,8},{8,10},{10,12},{12,14},{1,3},{3,5},{5,7},{... | collective-permute-start | bytes 196616 | tf_op jit(solution)/shard_map/ppermute | solution.py:12
  14.0 6.2 %collective-permute-start.1 = (bf16[128,256]{1,0:T(8,128)(2,1)S(1)}, bf16[128,256]{1,0:T(8,128)(2,1)S(1)}, u32[]{:S(2)}, u32[]{:S(2)}) collective-permute-start(bf16[128,256]{1,0:T(8,128)(2,1)S(1)} %gather_fusion.1), channel_id=1, source_target_pairs={{2,0},{4,2},{6,4},{8,6},{10,8},{12,10},{14,12},{3,1},{5,3},{7,5},{... | collective-permute-start | bytes 196616 | tf_op jit(solution)/shard_map/ppermute | solution.py:12
  16.7 3.6 %copy-start.8 = (f32[128]{0:T(128)}, f32[128]{0:T(128)S(1)}, u32[]{:S(2)}) copy-start(f32[128]{0:T(128)S(1)} %get-tuple-element.10) | copy-start | bytes 1540
  17.8 2.5 %copy-start.5 = (f32[1,1024,256]{2,1,0:T(8,128)}, f32[1,1024,256]{2,1,0:T(8,128)S(1)}, u32[]{:S(2)}) copy-start(f32[1,1024,256]{2,1,0:T(8,128)S(1)} %convert_element_type.57) | copy-start | bytes 3145732
  17.9 3.2 %copy-start.7 = (bf16[768,256]{1,0:T(8,128)(2,1)}, bf16[768,256]{1,0:T(8,128)(2,1)S(1)}, u32[]{:S(2)}) copy-start(bf16[768,256]{1,0:T(8,128)(2,1)S(1)} %fusion.23) | copy-start | bytes 1179652
  20.3 1.8 %copy-start.4 = (bf16[1,1024,128]{2,1,0:T(8,128)(2,1)S(1)}, bf16[1,1024,128]{2,1,0:T(8,128)(2,1)}, u32[]{:S(2)}) copy-start(bf16[1,1024,128]{2,1,0:T(8,128)(2,1)} %param.11) | copy-start | bytes 786436
  20.3 10.9 %copy-start.6 = (bf16[4,1,64,1,256]{4,2,3,1,0:T(8,128)(2,1)S(1)}, bf16[4,1,64,1,256]{4,2,3,1,0:T(8,128)(2,1)}, u32[]{:S(2)}) copy-start(bf16[4,1,64,1,256]{4,2,3,1,0:T(8,128)(2,1)} %param.13) | copy-start | bytes 393220
  21.1 1.0 copy-start.1
  32.4 75.4 %reduce-scatter.9.cloned.1.call-start = ((), (), s32[]{:S(2)}) async-start(), calls=%async_computation.5 | async-start | bytes 327680
  65.0 5.6 %collective-permute-start.2 = (bf16[128,256]{1,0:T(8,128)(2,1)}, bf16[128,256]{1,0:T(8,128)(2,1)S(1)}, u32[]{:S(2)}, u32[]{:S(2)}) collective-permute-start(bf16[128,256]{1,0:T(8,128)(2,1)} %gather_fusion.2), channel_id=1, source_target_pairs={{0,2},{2,4},{4,6},{6,8},{8,10},{10,12},{12,14},{1,3},{3,5},{5,7},{... | collective-permute-start | bytes 196616 | tf_op jit(solution)/shard_map/ppermute | solution.py:12
  68.5 6.4 %collective-permute-start.3 = (bf16[128,256]{1,0:T(8,128)(2,1)}, bf16[128,256]{1,0:T(8,128)(2,1)S(1)}, u32[]{:S(2)}, u32[]{:S(2)}) collective-permute-start(bf16[128,256]{1,0:T(8,128)(2,1)} %gather_fusion.3), channel_id=1, source_target_pairs={{2,0},{4,2},{6,4},{8,6},{10,8},{12,10},{14,12},{3,1},{5,3},{7,5},{... | collective-permute-start | bytes 196616 | tf_op jit(solution)/shard_map/ppermute | solution.py:12
  77.7 1.0 copy-start.2
  80.6 33.6 %copy-start.3 = (f32[1024,256]{0,1:T(8,128)S(1)}, f32[1024,256]{0,1:T(8,128)}, u32[]{:S(2)}) copy-start(f32[1024,256]{0,1:T(8,128)} %copy-done.2) | copy-start | bytes 3145732
Sparse Core Ops, SparseCore 0:
  32.5 20.0 reduce-scatter.6
  89.9 17.9 reduce-scatter.8
where the time goes:
time: 125 us; the launch traced here: 124 us
  waiting for transfers between devices  45.6 us (36%)
  blocking collectives  25.5 us (20%)
  local copies, waits for them, and re-layouts  17.6 us (14%)
  between operations  14.3 us (11%)
  starting transfers between devices  10.9 us (9%)
  matrix products  7.14 us (6%)
  other arithmetic  3.16 us (3%)
    unnamed x4, waiting for transfers between devices  38.3 us
    all_gather x2, blocking collectives, local(): lax.all_gather(all_modes, 'tile', axis=0, tiled=True)  13.3 us
    ppermute x4, starting transfers between devices, passed_along(): return lax.ppermute(shard, axis, pairs)  10.9 us
    all_to_all x2, blocking collectives, local(): lax.all_to_all(own_coarse, 'rep', split_axis=1, concat_axis=0, tiled=True)  8.49 us
    ppermute x4, waiting for transfers between devices, passed_along(): return lax.ppermute(shard, axis, pairs)  7.31 us
    unnamed x22, local copies, waits for them, and re-layouts  6.19 us
    all_gather x2, blocking collectives, local(): all_modes = lax.all_gather(projected, 'rep', axis=1, tiled=True)  3.79 us
    gather x2, local copies, waits for them, and re-layouts, local(): upper_trace = iterate[trace_rows[0, 1]]  3.33 us
  transfers between devices with their start and end apart: 6, of which 5 were waited for; matrix products, arithmetic and copies ran while one was open for 2% of the time, Pallas kernels for 0%

commit v1 on v0

v1 whole, which is shorter than its diff:
```python
import functools

import jax
import jax.numpy as jnp
from jax import lax
from jax.experimental import pallas as pl
from jax.experimental.pallas import tpu as pltpu
from jax.sharding import PartitionSpec as P

MESH = pl.DeviceIdType.MESH
ROW_TILES = 4
BF16 = jnp.bfloat16
F32 = jnp.float32


def mm(a, b):
    return jnp.dot(a, b, preferred_element_type=F32)


def middle_first(n):
    return sorted(range(1, n), key=lambda k: abs(2 * k - n))


def kernel(
    n_sub,
    n_tile,
    n_rep,
    source_hbm,
    inverse_hbm,
    coupling_ref,
    rows_ref,
    basis_hbm,
    counts_ref,
    coarse_hbm,
    out_hbm,
    source,
    inverse,
    basis,
    basis_t,
    coarse,
    solve,
    face_inverse,
    picked,
    blocks,
    shares,
    arrived,
    traces,
    halo,
    out,
    load_sem,
    inverse_sem,
    out_sem,
    rep_send,
    rep_recv,
    tile_send,
    tile_recv,
    sub_send,
    sub_recv,
    halo_send,
    halo_recv,
):
    j = lax.axis_index("sub")
    t = lax.axis_index("tile")
    r = lax.axis_index("rep")
    s = j * n_tile + t
    n_all = n_sub * n_tile
    slots = basis.shape[1]
    face = halo.shape[1]
    iface = source.shape[0]
    half = coarse_hbm.shape[1]
    chunk = iface // ROW_TILES

    has_lower = s > 0
    has_upper = s < n_all - 1
    below = lax.rem(s + n_all - 1, n_all)
    above = lax.rem(s + 1, n_all)
    lower_id = {"sub": lax.div(below, n_tile), "tile": lax.rem(below, n_tile)}
    upper_id = {"sub": lax.div(above, n_tile), "tile": lax.rem(above, n_tile)}

    def at_offset(axis, me, n, k):
        return {axis: lax.rem(me + k, n)}

    half_rows = pl.ds(pl.multiple_of(r * half, half), half)
    load_basis = pltpu.make_async_copy(basis_hbm, basis, load_sem.at[0])
    load_source = pltpu.make_async_copy(source_hbm, source, load_sem.at[1])
    load_coarse = pltpu.make_async_copy(coarse_hbm, coarse.at[:, half_rows, :], load_sem.at[2])
    load_basis.start()
    load_source.start()
    loads = []
    for i in range(ROW_TILES):
        part = pl.ds(i * chunk, chunk)
        loads.append(pltpu.make_async_copy(inverse_hbm.at[part], inverse.at[part], inverse_sem.at[i]))
        loads[-1].start()
    load_coarse.start()

    barrier = pltpu.get_barrier_semaphore()
    peers = [at_offset("rep", r, n_rep, k) for k in range(1, n_rep)]
    peers += [at_offset("tile", t, n_tile, k) for k in range(1, n_tile)]
    peers += [at_offset("sub", j, n_sub, k) for k in range(1, n_sub)]
    peers += [lower_id, upper_id]
    for peer in peers:
        pl.semaphore_signal(barrier, inc=1, device_id=peer, device_id_type=MESH)

    load_basis.wait()
    slot_ids = lax.broadcasted_iota(jnp.int32, (iface, slots), 1)
    live = slot_ids < counts_ref[0]
    basis[...] = jnp.where(live, basis[...].astype(F32), 0.0).astype(BF16)
    basis_t[...] = basis[...].astype(F32).T.astype(BF16)

    pl.semaphore_wait(barrier, len(peers))
    rep_copies = []
    for k in range(1, n_rep):
        copy = pltpu.make_async_remote_copy(
            src_ref=coarse_hbm,
            dst_ref=coarse.at[:, half_rows, :],
            send_sem=rep_send.at[k],
            recv_sem=rep_recv.at[k],
            device_id=at_offset("rep", r, n_rep, k),
            device_id_type=MESH,
        )
        copy.start()
        rep_copies.append(copy)

    load_source.wait()
    projected = jnp.zeros((slots, source.shape[1]), F32)
    for i in range(ROW_TILES):
        part = pl.ds(i * chunk, chunk)
        loads[i].wait()
        piece = mm(inverse[part, :], source[...])
        solve[part, :] = piece
        projected += mm(basis_t[:, part], piece.astype(BF16))

    def start_blocks(which, value):
        mine = pl.ds(pl.multiple_of(t * slots, slots), slots)
        blocks[which, mine, :] = value.astype(BF16)
        copies = []
        for k in range(1, n_tile):
            copy = pltpu.make_async_remote_copy(
                src_ref=blocks.at[which, mine],
                dst_ref=blocks.at[which, mine],
                send_sem=tile_send.at[which, k],
                recv_sem=tile_recv.at[which, k],
                device_id=at_offset("tile", t, n_tile, k),
                device_id_type=MESH,
            )
            copy.start()
            copies.append(copy)
        return copies

    def start_shares(which):
        copies = []
        for k in middle_first(n_sub):
            target = lax.rem(j + k, n_sub)
            shares[which, k] = mm(coarse[target], blocks[which]).astype(BF16)
            copy = pltpu.make_async_remote_copy(
                src_ref=shares.at[which, k],
                dst_ref=arrived.at[which, k],
                send_sem=sub_send.at[which, k],
                recv_sem=sub_recv.at[which, k],
                device_id=at_offset("sub", j, n_sub, k),
                device_id_type=MESH,
            )
            copy.start()
            copies.append(copy)
        return copies, mm(coarse[j], blocks[which])

    def summed(which, copies, total):
        for k, copy in zip(middle_first(n_sub), copies):
            copy.wait_recv()
            total += arrived[which, k].astype(F32)
        return total.astype(BF16)

    sends = list(rep_copies)
    tile_copies = start_blocks(0, projected)
    sends += tile_copies
    load_coarse.wait()
    face_inverse[:, :face] = (inverse[:, :face].astype(F32) * coupling_ref[0:1, :]).astype(BF16)
    face_inverse[:, face:] = (inverse[:, iface - face :].astype(F32) * coupling_ref[1:2, :]).astype(BF16)
    for copy in rep_copies + tile_copies:
        copy.wait_recv()
    sub_copies, total = start_shares(0)
    sends += sub_copies

    row_ids = lax.broadcasted_iota(jnp.int32, (iface, face), 0)
    for f in range(2):
        chosen = jnp.where(row_ids == rows_ref[f : f + 1, :], 1.0, 0.0)
        picked[pl.ds(f * face, face), :] = chosen.T.astype(BF16)
    trace_solve = mm(picked[...], solve[...].astype(BF16))
    trace_basis = mm(picked[...], basis[...]).astype(BF16)
    gram = mm(basis_t[...], basis[...]).astype(BF16)
    face_product = mm(basis_t[...], face_inverse[...]).astype(BF16)

    own = summed(0, sub_copies, total)
    traces[...] = (trace_solve + mm(trace_basis, own)).astype(BF16)

    to_upper = pltpu.make_async_remote_copy(
        src_ref=traces.at[pl.ds(face, face)],
        dst_ref=halo.at[0],
        send_sem=halo_send.at[0],
        recv_sem=halo_recv.at[0],
        device_id=upper_id,
        device_id_type=MESH,
    )
    to_lower = pltpu.make_async_remote_copy(
        src_ref=traces.at[pl.ds(0, face)],
        dst_ref=halo.at[1],
        send_sem=halo_send.at[1],
        recv_sem=halo_recv.at[1],
        device_id=lower_id,
        device_id_type=MESH,
    )

    @pl.when(has_upper)
    def _():
        to_upper.start()

    @pl.when(has_lower)
    def _():
        to_lower.start()

    @pl.when(jnp.logical_not(has_lower))
    def _():
        halo[0] = jnp.zeros(halo.shape[1:], BF16)

    @pl.when(jnp.logical_not(has_upper))
    def _():
        halo[1] = jnp.zeros(halo.shape[1:], BF16)

    step = mm(gram, own)

    @pl.when(has_lower)
    def _():
        to_upper.wait_recv()

    @pl.when(has_upper)
    def _():
        to_lower.wait_recv()

    projected = mm(face_product[:, :face], halo[0]) + mm(face_product[:, face:], halo[1]) - step
    tile_copies = start_blocks(1, projected)
    sends += tile_copies
    for copy in tile_copies:
        copy.wait_recv()
    sub_copies, total = start_shares(1)
    sends += sub_copies
    for i in range(ROW_TILES):
        part = pl.ds(i * chunk, chunk)
        solve[part, :] = (
            solve[part, :]
            + mm(face_inverse[part, :face], halo[0])
            + mm(face_inverse[part, face:], halo[1])
        )
    own = summed(1, sub_copies, total)
    stores = []
    for i in range(ROW_TILES):
        part = pl.ds(i * chunk, chunk)
        out[part, :] = (solve[part, :] + mm(basis[part, :], own)).astype(BF16)
        stores.append(pltpu.make_async_copy(out.at[part], out_hbm.at[part], out_sem.at[i]))
        stores[-1].start()

    @pl.when(has_upper)
    def _():
        to_upper.wait_send()

    @pl.when(has_lower)
    def _():
        to_lower.wait_send()

    for copy in sends:
        copy.wait_send()
    for store in stores:
        store.wait()


def local(
    n_sub,
    n_tile,
    n_rep,
    right_side,
    interface_inverse,
    coupling,
    trace_rows,
    deflation_basis,
    deflation_counts,
    coarse_inverse,
):
    source = right_side[0]
    iface, modes = source.shape
    face = coupling.shape[2]
    slots = deflation_basis.shape[2]
    half = coarse_inverse.shape[2]
    inputs = coarse_inverse.shape[4]
    coarse_block = coarse_inverse.reshape(n_sub, half, inputs)
    hbm = pl.BlockSpec(memory_space=pl.ANY)
    vmem = pl.BlockSpec(memory_space=pltpu.VMEM)
    smem = pl.BlockSpec(memory_space=pltpu.SMEM)
    dma = pltpu.SemaphoreType.DMA
    macs = modes * (iface * iface + 6 * iface * slots + 2 * n_sub * slots * inputs)
    field = pl.pallas_call(
        functools.partial(kernel, n_sub, n_tile, n_rep),
        out_shape=jax.ShapeDtypeStruct((iface, modes), BF16),
        in_specs=[hbm, hbm, vmem, vmem, hbm, smem, hbm],
        out_specs=hbm,
        scratch_shapes=[
            pltpu.VMEM((iface, modes), BF16),
            pltpu.VMEM((iface, iface), BF16),
            pltpu.VMEM((iface, slots), BF16),
            pltpu.VMEM((slots, iface), BF16),
            pltpu.VMEM((n_sub, slots, inputs), BF16),
            pltpu.VMEM((iface, modes), F32),
            pltpu.VMEM((iface, 2 * face), BF16),
            pltpu.VMEM((2 * face, iface), BF16),
            pltpu.VMEM((2, inputs, modes), BF16),
            pltpu.VMEM((2, n_sub, slots, modes), BF16),
            pltpu.VMEM((2, n_sub, slots, modes), BF16),
            pltpu.VMEM((2 * face, modes), BF16),
            pltpu.VMEM((2, face, modes), BF16),
            pltpu.VMEM((iface, modes), BF16),
            dma((3,)),
            dma((ROW_TILES,)),
            dma((ROW_TILES,)),
            dma((n_rep,)),
            dma((n_rep,)),
            dma((2, n_tile)),
            dma((2, n_tile)),
            dma((2, n_sub)),
            dma((2, n_sub)),
            dma((2,)),
            dma((2,)),
        ],
        compiler_params=pltpu.CompilerParams(
            collective_id=0, has_side_effects=True, vmem_limit_bytes=56 * 1024 * 1024
        ),
        cost_estimate=pl.CostEstimate(
            flops=2 * macs, bytes_accessed=2 * iface * (iface + 2 * modes + slots), transcendentals=0
        ),
    )(
        source,
        interface_inverse[0],
        coupling[0],
        trace_rows[0],
        deflation_basis[0],
        deflation_counts,
        coarse_block,
    )
    return field[None]


def solution(mesh):
    placed = (
        P(("group", "sub", "tile"), None, "rep"),
        P(("group", "sub", "tile"), None, None),
        P(("group", "sub", "tile"), None, None),
        P(("group", "sub", "tile"), None, None),
        P(("group", "sub", "tile"), None, None),
        P(("group", "sub", "tile")),
        P("group", "tile", "rep", "sub", None),
    )
    return jax.shard_map(
        functools.partial(local, mesh.shape["sub"], mesh.shape["tile"], mesh.shape["rep"]),
        mesh=mesh,
        in_specs=placed,
        out_specs=P(("group", "sub", "tile"), None, "rep"),
        check_vma=False,
    )
```

time: 125 us -> 35.3 us (0.28)
  waiting for transfers between devices: 45.6 us -> 0 us
  Pallas kernels: 0 us -> 32.6 us
  blocking collectives: 25.5 us -> 0 us
  local copies, waits for them, and re-layouts: 17.6 us -> 1.87 us
  between operations: 14.3 us -> 0.66 us
  starting transfers between devices: 10.9 us -> 0 us
  matrix products: 7.14 us -> 0 us
  other arithmetic: 3.16 us -> 0 us
    unnamed x4 -> x0, waiting for transfers between devices: 38.3 us -> none
    pallas_call x0 -> x1, Pallas kernels: none -> 32.6 us  [local(): pl.pallas_call(functools.partial(kernel, n_sub, n_tile, n_rep), out_shape...]
    all_gather x4 -> x0, blocking collectives: 17.1 us -> none  [the longest x2 13.3 us: local(): lax.all_gather(all_modes, 'tile', axis=0, tiled=True)]
    ppermute x4 -> x0, starting transfers between devices: 10.9 us -> none  [passed_along(): return lax.ppermute(shard, axis, pairs)]
    all_to_all x2 -> x0, blocking collectives: 8.49 us -> none  [local(): lax.all_to_all(own_coarse, 'rep', split_axis=1, concat_axis=0, tiled=True)]
    ppermute x4 -> x0, waiting for transfers between devices: 7.31 us -> none  [passed_along(): return lax.ppermute(shard, axis, pairs)]
    dot_general x8 -> x0, matrix products: 7.14 us -> none  [the longest x2 2.69 us: local(): jnp.dot(masked_basis, coarse_rows, preferred_element_type=jnp.float32)]
    gather x4 -> x0, local copies, waits for them, and re-layouts: 6.66 us -> none  [the longest x2 3.33 us: local(): upper_trace = iterate[trace_rows[0, 1]]]
  transfers between devices with their start and end apart: 6 -> 0, of which waited for: 5 -> 0; matrix products, arithmetic and copies ran while one was open for 2% -> 0% of each run, Pallas kernels for 0% -> 0%
where the time goes in v1:
time: 35.3 us; the launch traced here: 35.1 us
  Pallas kernels  32.6 us (92%)
  local copies, waits for them, and re-layouts  1.87 us (5%)
  between operations  0.66 us (2%)
    pallas_call x1, Pallas kernels, local(): pl.pallas_call(functools.partial(kernel, n_sub, n_tile, n_rep), out_shape...  32.6 us
    unnamed x1, local copies, waits for them, and re-layouts  1.87 us

profile of v1, /device:TPU:0, one launch (start us, length us, event | category | flops | bytes accessed | tf_op | source)
XLA Modules:
  0.0 35.1 jit_solution(500708250420709001)
XLA Ops:
  0.7 32.6 %shard_map.73 = bf16[1024,256]{1,0:T(8,128)(2,1)} custom-call(bf16[1024,256]{1,0:T(8,128)(2,1)} %bitcast.9, bf16[1024,1024]{1,0:T(8,128)(2,1)} %bitcast.8, f32[2,128]{1,0:T(2,128)} %bitcast.12, s32[2,128]{1,0:T(2,128)} %bitcast.13, bf16[1024,128]{1,0:T(8,128)(2,1)} %bitcast.10, s32[1]{0:T(128)S(6)} %copy.9.counts_ref, bf16[4,64,256]{2,1,0:T(8,128)(2,1)} %bitcast.11), custom_call_target="tpu_custom_call" | custom-call | flops 1073741824 | bytes 3407872 | tf_op jit(solution)/shard_map/pallas_call | solution.py:299
  33.2 1.9 %copy.10 = bf16[1,1024,256]{2,1,0:T(8,128)(2,1)} copy(bf16[1,1024,256]{2,1,0:T(8,128)(2,1)} %bitcast.7) | data formatting | bytes 1048576

commit v2 on v1

--- a/solution.py
+++ b/solution.py
@@ -25,6 +25,7 @@
     n_sub,
     n_tile,
     n_rep,
+    pack,
     source_hbm,
     inverse_hbm,
     coupling_ref,
@@ -52,8 +53,12 @@
     out_sem,
     rep_send,
     rep_recv,
-    tile_send,
-    tile_recv,
+    relay_send,
+    relay_recv,
+    pack_send,
+    pack_recv,
+    block_send,
+    block_recv,
     sub_send,
     sub_recv,
     halo_send,
@@ -67,7 +72,11 @@
     slots = basis.shape[1]
     face = halo.shape[1]
     iface = source.shape[0]
-    half = coarse_hbm.shape[1]
+    half = coarse_hbm.shape[2]
+    inputs = coarse_hbm.shape[3]
+    n_packs = n_sub // pack
+    mine = lax.div(j, pack)
+    i = lax.rem(j, pack)
     chunk = iface // ROW_TILES
 
     has_lower = s > 0
@@ -77,26 +86,39 @@
     lower_id = {"sub": lax.div(below, n_tile), "tile": lax.rem(below, n_tile)}
     upper_id = {"sub": lax.div(above, n_tile), "tile": lax.rem(above, n_tile)}
 
-    def at_offset(axis, me, n, k):
-        return {axis: lax.rem(me + k, n)}
+    def rep_id(k):
+        return {"rep": lax.rem(r + k, n_rep)}
+
+    def pack_id(k, k_tile):
+        return {"sub": mine * pack + lax.rem(i + k, pack), "tile": lax.rem(t + k_tile, n_tile)}
+
+    def share_id(k):
+        return {"sub": lax.rem(mine + k, n_packs) * pack + i}
+
+    def pack_columns(k):
+        return pl.ds(pl.multiple_of(lax.rem(i + k, pack) * inputs, inputs), inputs)
+
+    square = [(a, b) for a in range(pack) for b in range(n_tile) if a or b][::-1]
 
     half_rows = pl.ds(pl.multiple_of(r * half, half), half)
     load_basis = pltpu.make_async_copy(basis_hbm, basis, load_sem.at[0])
     load_source = pltpu.make_async_copy(source_hbm, source, load_sem.at[1])
-    load_coarse = pltpu.make_async_copy(coarse_hbm, coarse.at[:, half_rows, :], load_sem.at[2])
+    load_coarse = pltpu.make_async_copy(
+        coarse_hbm.at[:, i], coarse.at[:, half_rows, pack_columns(0)], load_sem.at[2]
+    )
     load_basis.start()
     load_source.start()
     loads = []
-    for i in range(ROW_TILES):
-        part = pl.ds(i * chunk, chunk)
-        loads.append(pltpu.make_async_copy(inverse_hbm.at[part], inverse.at[part], inverse_sem.at[i]))
+    for q in range(ROW_TILES):
+        part = pl.ds(q * chunk, chunk)
+        loads.append(pltpu.make_async_copy(inverse_hbm.at[part], inverse.at[part], inverse_sem.at[q]))
         loads[-1].start()
     load_coarse.start()
 
     barrier = pltpu.get_barrier_semaphore()
-    peers = [at_offset("rep", r, n_rep, k) for k in range(1, n_rep)]
-    peers += [at_offset("tile", t, n_tile, k) for k in range(1, n_tile)]
-    peers += [at_offset("sub", j, n_sub, k) for k in range(1, n_sub)]
+    peers = [rep_id(k) for k in range(1, n_rep)]
+    peers += [pack_id(a, b) for a, b in square]
+    peers += [share_id(k) for k in range(1, n_packs)]
     peers += [lower_id, upper_id]
     for peer in peers:
         pl.semaphore_signal(barrier, inc=1, device_id=peer, device_id_type=MESH)
@@ -108,14 +130,26 @@
     basis_t[...] = basis[...].astype(F32).T.astype(BF16)
 
     pl.semaphore_wait(barrier, len(peers))
+    pack_copies = []
+    for k in range(1, pack):
+        copy = pltpu.make_async_remote_copy(
+            src_ref=coarse_hbm.at[:, lax.rem(i + k, pack)],
+            dst_ref=coarse.at[:, half_rows, pack_columns(0)],
+            send_sem=pack_send.at[k],
+            recv_sem=pack_recv.at[k],
+            device_id=pack_id(k, 0),
+            device_id_type=MESH,
+        )
+        copy.start()
+        pack_copies.append(copy)
     rep_copies = []
     for k in range(1, n_rep):
         copy = pltpu.make_async_remote_copy(
-            src_ref=coarse_hbm,
-            dst_ref=coarse.at[:, half_rows, :],
+            src_ref=coarse_hbm.at[:, i],
+            dst_ref=coarse.at[:, half_rows, pack_columns(0)],
             send_sem=rep_send.at[k],
             recv_sem=rep_recv.at[k],
-            device_id=at_offset("rep", r, n_rep, k),
+            device_id=rep_id(k),
             device_id_type=MESH,
         )
         copy.start()
@@ -123,24 +157,24 @@
 
     load_source.wait()
     projected = jnp.zeros((slots, source.shape[1]), F32)
-    for i in range(ROW_TILES):
-        part = pl.ds(i * chunk, chunk)
-        loads[i].wait()
+    for q in range(ROW_TILES):
+        part = pl.ds(q * chunk, chunk)
+        loads[q].wait()
         piece = mm(inverse[part, :], source[...])
         solve[part, :] = piece
         projected += mm(basis_t[:, part], piece.astype(BF16))
 
     def start_blocks(which, value):
-        mine = pl.ds(pl.multiple_of(t * slots, slots), slots)
-        blocks[which, mine, :] = value.astype(BF16)
+        place = pl.ds(pl.multiple_of((i * n_tile + t) * slots, slots), slots)
+        blocks[which, place, :] = value.astype(BF16)
         copies = []
-        for k in range(1, n_tile):
+        for a, b in square:
             copy = pltpu.make_async_remote_copy(
-                src_ref=blocks.at[which, mine],
-                dst_ref=blocks.at[which, mine],
-                send_sem=tile_send.at[which, k],
-                recv_sem=tile_recv.at[which, k],
-                device_id=at_offset("tile", t, n_tile, k),
+                src_ref=blocks.at[which, place],
+                dst_ref=blocks.at[which, place],
+                send_sem=block_send.at[which, a, b],
+                recv_sem=block_recv.at[which, a, b],
+                device_id=pack_id(a, b),
                 device_id_type=MESH,
             )
             copy.start()
@@ -149,34 +183,50 @@
 
     def start_shares(which):
         copies = []
-        for k in middle_first(n_sub):
-            target = lax.rem(j + k, n_sub)
+        for k in middle_first(n_packs):
+            target = lax.rem(mine + k, n_packs)
             shares[which, k] = mm(coarse[target], blocks[which]).astype(BF16)
             copy = pltpu.make_async_remote_copy(
                 src_ref=shares.at[which, k],
                 dst_ref=arrived.at[which, k],
                 send_sem=sub_send.at[which, k],
                 recv_sem=sub_recv.at[which, k],
-                device_id=at_offset("sub", j, n_sub, k),
+                device_id=share_id(k),
                 device_id_type=MESH,
             )
             copy.start()
             copies.append(copy)
-        return copies, mm(coarse[j], blocks[which])
+        return copies, mm(coarse[mine], blocks[which])
 
     def summed(which, copies, total):
-        for k, copy in zip(middle_first(n_sub), copies):
+        for k, copy in zip(middle_first(n_packs), copies):
             copy.wait_recv()
             total += arrived[which, k].astype(F32)
         return total.astype(BF16)
 
-    sends = list(rep_copies)
-    tile_copies = start_blocks(0, projected)
-    sends += tile_copies
+    sends = rep_copies + pack_copies
+    block_copies = start_blocks(0, projected)
+    sends += block_copies
+    relays = []
+    for k, arriving in zip(range(1, pack), pack_copies):
+        arriving.wait_recv()
+        piece = coarse.at[:, half_rows, pack_columns(pack - k)]
+        for m in range(1, n_rep):
+            copy = pltpu.make_async_remote_copy(
+                src_ref=piece,
+                dst_ref=piece,
+                send_sem=relay_send.at[k, m],
+                recv_sem=relay_recv.at[k, m],
+                device_id=rep_id(m),
+                device_id_type=MESH,
+            )
+            copy.start()
+            relays.append(copy)
+    sends += relays
     load_coarse.wait()
     face_inverse[:, :face] = (inverse[:, :face].astype(F32) * coupling_ref[0:1, :]).astype(BF16)
     face_inverse[:, face:] = (inverse[:, iface - face :].astype(F32) * coupling_ref[1:2, :]).astype(BF16)
-    for copy in rep_copies + tile_copies:
+    for copy in rep_copies + relays + block_copies:
         copy.wait_recv()
     sub_copies, total = start_shares(0)
     sends += sub_copies
@@ -237,14 +287,14 @@
         to_lower.wait_recv()
 
     projected = mm(face_product[:, :face], halo[0]) + mm(face_product[:, face:], halo[1]) - step
-    tile_copies = start_blocks(1, projected)
-    sends += tile_copies
-    for copy in tile_copies:
+    block_copies = start_blocks(1, projected)
+    sends += block_copies
+    for copy in block_copies:
         copy.wait_recv()
     sub_copies, total = start_shares(1)
     sends += sub_copies
-    for i in range(ROW_TILES):
-        part = pl.ds(i * chunk, chunk)
+    for q in range(ROW_TILES):
+        part = pl.ds(q * chunk, chunk)
         solve[part, :] = (
             solve[part, :]
             + mm(face_inverse[part, :face], halo[0])
@@ -252,10 +302,10 @@
         )
     own = summed(1, sub_copies, total)
     stores = []
-    for i in range(ROW_TILES):
-        part = pl.ds(i * chunk, chunk)
+    for q in range(ROW_TILES):
+        part = pl.ds(q * chunk, chunk)
         out[part, :] = (solve[part, :] + mm(basis[part, :], own)).astype(BF16)
-        stores.append(pltpu.make_async_copy(out.at[part], out_hbm.at[part], out_sem.at[i]))
+        stores.append(pltpu.make_async_copy(out.at[part], out_hbm.at[part], out_sem.at[q]))
         stores[-1].start()
 
     @pl.when(has_upper)
@@ -290,14 +340,16 @@
     slots = deflation_basis.shape[2]
     half = coarse_inverse.shape[2]
     inputs = coarse_inverse.shape[4]
-    coarse_block = coarse_inverse.reshape(n_sub, half, inputs)
+    pack = 2 if n_sub % 2 == 0 else 1
+    n_packs = n_sub // pack
+    coarse_block = coarse_inverse.reshape(n_packs, pack, half, inputs)
     hbm = pl.BlockSpec(memory_space=pl.ANY)
     vmem = pl.BlockSpec(memory_space=pltpu.VMEM)
     smem = pl.BlockSpec(memory_space=pltpu.SMEM)
     dma = pltpu.SemaphoreType.DMA
     macs = modes * (iface * iface + 6 * iface * slots + 2 * n_sub * slots * inputs)
     field = pl.pallas_call(
-        functools.partial(kernel, n_sub, n_tile, n_rep),
+        functools.partial(kernel, n_sub, n_tile, n_rep, pack),
         out_shape=jax.ShapeDtypeStruct((iface, modes), BF16),
         in_specs=[hbm, hbm, vmem, vmem, hbm, smem, hbm],
         out_specs=hbm,
@@ -306,13 +358,13 @@
             pltpu.VMEM((iface, iface), BF16),
             pltpu.VMEM((iface, slots), BF16),
             pltpu.VMEM((slots, iface), BF16),
-            pltpu.VMEM((n_sub, slots, inputs), BF16),
+            pltpu.VMEM((n_packs, slots, pack * inputs), BF16),
             pltpu.VMEM((iface, modes), F32),
             pltpu.VMEM((iface, 2 * face), BF16),
             pltpu.VMEM((2 * face, iface), BF16),
-            pltpu.VMEM((2, inputs, modes), BF16),
-            pltpu.VMEM((2, n_sub, slots, modes), BF16),
-            pltpu.VMEM((2, n_sub, slots, modes), BF16),
+            pltpu.VMEM((2, pack * inputs, modes), BF16),
+            pltpu.VMEM((2, n_packs, slots, modes), BF16),
+            pltpu.VMEM((2, n_packs, slots, modes), BF16),
             pltpu.VMEM((2 * face, modes), BF16),
             pltpu.VMEM((2, face, modes), BF16),
             pltpu.VMEM((iface, modes), BF16),
@@ -321,10 +373,14 @@
             dma((ROW_TILES,)),
             dma((n_rep,)),
             dma((n_rep,)),
-            dma((2, n_tile)),
-            dma((2, n_tile)),
-            dma((2, n_sub)),
-            dma((2, n_sub)),
+            dma((pack, n_rep)),
+            dma((pack, n_rep)),
+            dma((pack,)),
+            dma((pack,)),
+            dma((2, pack, n_tile)),
+            dma((2, pack, n_tile)),
+            dma((2, n_packs)),
+            dma((2, n_packs)),
             dma((2,)),
             dma((2,)),
         ],

time: 35.3 us -> 35.9 us (1.017)
  Pallas kernels: 32.6 us -> 33.2 us
    pallas_call x1, Pallas kernels: 32.6 us -> 33.2 us  [local(): pl.pallas_call(functools.partial(kernel, n_sub, n_tile, n_rep, pack), out...]
where the time goes in v2:
time: 35.9 us; the launch traced here: 35.7 us
  Pallas kernels  33.2 us (92%)
  local copies, waits for them, and re-layouts  1.87 us (5%)
  between operations  0.66 us (2%)
    pallas_call x1, Pallas kernels, local(): pl.pallas_call(functools.partial(kernel, n_sub, n_tile, n_rep, pack), out...  33.2 us
    unnamed x1, local copies, waits for them, and re-layouts  1.87 us

profile of v2, /device:TPU:0, one launch (start us, length us, event | category | flops | bytes accessed | tf_op | source)
XLA Modules:
  0.0 35.7 jit_solution(9389395090888090508)
XLA Ops:
  0.7 33.2 %shard_map.73 = bf16[1024,256]{1,0:T(8,128)(2,1)} custom-call(bf16[1024,256]{1,0:T(8,128)(2,1)} %bitcast.9, bf16[1024,1024]{1,0:T(8,128)(2,1)} %bitcast.8, f32[2,128]{1,0:T(2,128)} %bitcast.12, s32[2,128]{1,0:T(2,128)} %bitcast.13, bf16[1024,128]{1,0:T(8,128)(2,1)} %bitcast.10, s32[1]{0:T(128)S(6)} %copy.9.counts_ref, bf16[2,2,64,256]{3,2,1,0:T(8,128)(2,1)} %bitcast.11), custom_call_target="tpu_custom_call" | custom-call | flops 1073741824 | bytes 3407872 | tf_op jit(solution)/shard_map/pallas_call | solution.py:351
  33.9 1.9 %copy.10 = bf16[1,1024,256]{2,1,0:T(8,128)(2,1)} copy(bf16[1,1024,256]{2,1,0:T(8,128)(2,1)} %bitcast.7) | data formatting | bytes 1048576
